TPU v7x, 128 devices: a whole 4x4x4 slice. The times are simulated.
128 devices in a mesh: fsdp: 16 (over z_hi, y, core), seq: 8 (over z_lo, x).
Axes of the slice: x: 4, y: 4, z: 4 (z_hi: 2, z_lo: 2; z = z_hi * 2 + z_lo), core: 2. Of those that a mesh axis runs over, the one named last changes fastest.
Arguments:
- tokens: bfloat16 [32768, 768], P(('fsdp', 'seq')), may hold values from -6 to 6
- lengths: int32 [16, 3], P('fsdp'), may hold values from 1 to 13, 16 in all within a row
- block_table: int32 [16, 16], P('fsdp'), may hold values from 0 to 15, each once within a row
- qkv_weight: bfloat16 [768, 2304], P(('fsdp', 'seq')), may hold values from -0.21875 to 0.21875
- query_bias: bfloat16 [768], P(('fsdp', 'seq')), may hold values from -3 to 3
- value_bias: bfloat16 [768], P(('fsdp', 'seq')), may hold values from -0.1796875 to 0.1796875
- out_weight: bfloat16 [768, 768], P(('fsdp', 'seq')), may hold values from -3 to 3
- out_bias: bfloat16 [768], P(('fsdp', 'seq')), may hold values from -2 to 2
- first_gain: bfloat16 [768], P(('fsdp', 'seq')), may hold values from 0.5 to 1.5
- first_shift: bfloat16 [768], P(('fsdp', 'seq')), may hold values from -2 to 2
- up_weight: bfloat16 [768, 3072], P(('fsdp', 'seq')), may hold values from -0.21875 to 0.21875
- up_bias: bfloat16 [3072], P(('fsdp', 'seq')), may hold values from -2 to 2
- down_weight: bfloat16 [3072, 768], P(('fsdp', 'seq')), may hold values from -0.109375 to 0.109375
- down_bias: bfloat16 [768], P(('fsdp', 'seq')), may hold values from -2 to 2
- second_gain: bfloat16 [768], P(('fsdp', 'seq')), may hold values from 0.5 to 1.5
- second_shift: bfloat16 [768], P(('fsdp', 'seq')), may hold values from -2 to 2
- cotangent: bfloat16 [32768, 768], P(('fsdp', 'seq')), may hold values from -6 to 6
Outputs:
- layer_out: bfloat16 [32768, 768], P(('fsdp', 'seq'))
- tokens_grad: float32 [32768, 768], P(('fsdp', 'seq'))
- qkv_weight_grad: float32 [768, 2304], P(('fsdp', 'seq'))
- query_bias_grad: float32 [768], P(('fsdp', 'seq'))
- value_bias_grad: float32 [768], P(('fsdp', 'seq'))
- out_weight_grad: float32 [768, 768], P(('fsdp', 'seq'))
- out_bias_grad: float32 [768], P(('fsdp', 'seq'))
- first_gain_grad: float32 [768], P(('fsdp', 'seq'))
- first_shift_grad: float32 [768], P(('fsdp', 'seq'))
- up_weight_grad: float32 [768, 3072], P(('fsdp', 'seq'))
- up_bias_grad: float32 [3072], P(('fsdp', 'seq'))
- down_weight_grad: float32 [3072, 768], P(('fsdp', 'seq'))
- down_bias_grad: float32 [768], P(('fsdp', 'seq'))
- second_gain_grad: float32 [768], P(('fsdp', 'seq'))
- second_shift_grad: float32 [768], P(('fsdp', 'seq'))
Inputs may be any that keep to these rules, and one draw needn't show every extreme that they name: `lengths`: each row sums to 16, and one entry of it is exactly 13. `block_table`: each row is a permutation of 0 to 15.
All inputs are finite; a program needn't handle non-finite values.
Results may differ from a plain program's by a relative error of at most 0.023.
Values may be sent and summed in bfloat16 or wider, within the bound.
A program may use at most 128 MiB of HBM per device.

v0:
```python
import math

import jax
import jax.numpy as jnp
from jax import lax
from jax.sharding import PartitionSpec as P

HD = 64


EPS = 1e-12


def normalize(z):
    centered = z - jnp.mean(z, axis=-1, keepdims=True)
    factor = lax.rsqrt(jnp.mean(centered * centered, axis=-1, keepdims=True) + EPS)
    return (centered * factor, factor)


def norm_back(grad_out, normed, factor, gain):
    scaled = grad_out * gain
    inner = jnp.mean(scaled * normed, axis=-1, keepdims=True)
    return factor * (scaled - jnp.mean(scaled, axis=-1, keepdims=True) - normed * inner)


def contract_rows(left, right):
    return lax.dot_general(
        left, right, (((0,), (0,)), ((), ())), preferred_element_type=jnp.float32
    )


def times_transpose(left, right):
    return lax.dot_general(
        left, right, (((1,), (1,)), ((), ())), preferred_element_type=jnp.float32
    )


def shards(
    tokens,
    lengths,
    block_table,
    qkv_weight,
    query_bias,
    value_bias,
    out_weight,
    out_bias,
    first_gain,
    first_shift,
    up_weight,
    up_bias,
    down_weight,
    down_bias,
    second_gain,
    second_shift,
    cotangent,
):
    full = (
        lax.all_gather(qkv_weight, ("fsdp", "seq"), axis=0, tiled=True),
        lax.all_gather(query_bias, ("fsdp", "seq"), axis=0, tiled=True),
        lax.all_gather(value_bias, ("fsdp", "seq"), axis=0, tiled=True),
        lax.all_gather(out_weight, ("fsdp", "seq"), axis=0, tiled=True),
        lax.all_gather(out_bias, ("fsdp", "seq"), axis=0, tiled=True),
        lax.all_gather(first_gain, ("fsdp", "seq"), axis=0, tiled=True),
        lax.all_gather(first_shift, ("fsdp", "seq"), axis=0, tiled=True),
        lax.all_gather(up_weight, ("fsdp", "seq"), axis=0, tiled=True),
        lax.all_gather(up_bias, ("fsdp", "seq"), axis=0, tiled=True),
        lax.all_gather(down_weight, ("fsdp", "seq"), axis=0, tiled=True),
        lax.all_gather(down_bias, ("fsdp", "seq"), axis=0, tiled=True),
        lax.all_gather(second_gain, ("fsdp", "seq"), axis=0, tiled=True),
        lax.all_gather(second_shift, ("fsdp", "seq"), axis=0, tiled=True),
    )
    (
        qkv_full,
        qbias_full,
        vbias_full,
        outw_full,
        outb_full,
        gain_one,
        shift_one,
        upw_full,
        upb_full,
        downw_full,
        downb_full,
        gain_two,
        shift_two,
    ) = full
    rows, width = tokens.shape
    heads = width // HD
    scale = 1.0 / math.sqrt(HD)
    group_rows = rows * lax.axis_size("seq")
    ends = jnp.cumsum(lengths[0])
    block_seg = jnp.sum((block_table[0][:, None] >= ends[None, :]).astype(jnp.int32), axis=1)
    key_seg = jnp.repeat(block_seg, group_rows // block_seg.shape[0])
    query_seg = lax.dynamic_slice_in_dim(key_seg, lax.axis_index("seq") * rows, rows)
    allowed = query_seg[:, None] == key_seg[None, :]

    def split_heads(m):
        return m.reshape(m.shape[0], heads, HD).transpose(1, 0, 2)

    def join_heads(m):
        return m.transpose(1, 0, 2).reshape(m.shape[1], width)

    inputs = tokens.astype(jnp.float32)
    qkv = jnp.dot(tokens, qkv_full, preferred_element_type=jnp.float32)
    query = (qkv[:, :width] + qbias_full.astype(jnp.float32)).astype(jnp.bfloat16)
    key = qkv[:, width : 2 * width].astype(jnp.bfloat16)
    value = (qkv[:, 2 * width :] + vbias_full.astype(jnp.float32)).astype(jnp.bfloat16)
    keys_all, values_all = (
        lax.all_gather(key, "seq", axis=0, tiled=True),
        lax.all_gather(value, "seq", axis=0, tiled=True),
    )
    q_heads = split_heads(query)
    k_heads = split_heads(keys_all)
    v_heads = split_heads(values_all)

    def attend(parts):
        q_head, k_head, v_head = parts
        scores = jnp.einsum("qd,kd->qk", q_head, k_head, preferred_element_type=jnp.float32) * scale
        scores = jnp.where(allowed, scores, -1e30)
        top = jnp.max(scores, axis=-1, keepdims=True)
        expo = jnp.exp(scores - top)
        total = jnp.sum(expo, axis=-1, keepdims=True)
        probs = (expo / total).astype(jnp.bfloat16)
        out = jnp.dot(probs, v_head, preferred_element_type=jnp.float32)
        return (out, top[:, 0] + jnp.log(total[:, 0]))

    o_heads, log_totals = lax.map(attend, (q_heads, k_heads, v_heads))
    attended = join_heads(o_heads).astype(jnp.bfloat16)
    branch = jnp.dot(attended, outw_full, preferred_element_type=jnp.float32) + outb_full.astype(
        jnp.float32
    )
    normed_one, factor_one = normalize(inputs + branch)
    gain_onef = gain_one.astype(jnp.float32)
    hidden_one = normed_one * gain_onef + shift_one.astype(jnp.float32)
    hidden_low = hidden_one.astype(jnp.bfloat16)
    upper = jnp.dot(hidden_low, upw_full, preferred_element_type=jnp.float32) + upb_full.astype(
        jnp.float32
    )
    activ, gelu_back = jax.vjp(jax.nn.gelu, upper)
    activ_low = activ.astype(jnp.bfloat16)
    feed = jnp.dot(activ_low, downw_full, preferred_element_type=jnp.float32) + downb_full.astype(
        jnp.float32
    )
    normed_two, factor_two = normalize(hidden_one + feed)
    gain_twof = gain_two.astype(jnp.float32)
    result = normed_two * gain_twof + shift_two.astype(jnp.float32)
    qkv_back, outw_back, upw_back, downw_back, gain_oneb, gain_twob = (
        lax.all_gather(qkv_weight, ("fsdp", "seq"), axis=0, tiled=True),
        lax.all_gather(out_weight, ("fsdp", "seq"), axis=0, tiled=True),
        lax.all_gather(up_weight, ("fsdp", "seq"), axis=0, tiled=True),
        lax.all_gather(down_weight, ("fsdp", "seq"), axis=0, tiled=True),
        lax.all_gather(first_gain, ("fsdp", "seq"), axis=0, tiled=True),
        lax.all_gather(second_gain, ("fsdp", "seq"), axis=0, tiled=True),
    )
    grad_out = cotangent.astype(jnp.float32)
    grad_ztwo = norm_back(grad_out, normed_two, factor_two, gain_twob.astype(jnp.float32))
    grad_gain_two = jnp.sum(grad_out * normed_two, axis=0)
    grad_shift_two = jnp.sum(grad_out, axis=0)
    grad_feed = grad_ztwo.astype(jnp.bfloat16)
    grad_downw = contract_rows(activ_low, grad_feed)
    grad_downb = jnp.sum(grad_feed.astype(jnp.float32), axis=0)
    grad_activ = times_transpose(grad_feed, downw_back)
    grad_upper = gelu_back(grad_activ)[0].astype(jnp.bfloat16)
    grad_upw = contract_rows(hidden_low, grad_upper)
    grad_upb = jnp.sum(grad_upper.astype(jnp.float32), axis=0)
    grad_hidden = grad_ztwo + times_transpose(grad_upper, upw_back)
    grad_zone = norm_back(grad_hidden, normed_one, factor_one, gain_oneb.astype(jnp.float32))
    grad_gain_one = jnp.sum(grad_hidden * normed_one, axis=0)
    grad_shift_one = jnp.sum(grad_hidden, axis=0)
    grad_branch = grad_zone.astype(jnp.bfloat16)
    grad_outw = contract_rows(attended, grad_branch)
    grad_outb = jnp.sum(grad_branch.astype(jnp.float32), axis=0)
    grad_attended = times_transpose(grad_branch, outw_back).astype(jnp.bfloat16)
    grad_heads = split_heads(grad_attended)

    def attend_back(parts):
        q_head, k_head, v_head, grad_head, log_total = parts
        scores = jnp.einsum("qd,kd->qk", q_head, k_head, preferred_element_type=jnp.float32) * scale
        probs = jnp.where(allowed, jnp.exp(scores - log_total[:, None]), 0.0)
        grad_probs = jnp.einsum("qd,kd->qk", grad_head, v_head, preferred_element_type=jnp.float32)
        inner = jnp.sum(probs * grad_probs, axis=-1, keepdims=True)
        grad_scores = (probs * (grad_probs - inner)).astype(jnp.bfloat16)
        grad_q = jnp.dot(grad_scores, k_head, preferred_element_type=jnp.float32) * scale
        grad_k = (
            jnp.einsum("qk,qd->kd", grad_scores, q_head, preferred_element_type=jnp.float32) * scale
        )
        grad_v = jnp.einsum(
            "qk,qd->kd", probs.astype(jnp.bfloat16), grad_head, preferred_element_type=jnp.float32
        )
        return (grad_q, grad_k, grad_v)

    grad_qh, grad_kh, grad_vh = lax.map(
        attend_back, (q_heads, k_heads, v_heads, grad_heads, log_totals)
    )
    grad_keys, grad_values = (
        lax.psum_scatter(
            join_heads(grad_kh).astype(jnp.bfloat16), "seq", scatter_dimension=0, tiled=True
        ).astype(jnp.float32),
        lax.psum_scatter(
            join_heads(grad_vh).astype(jnp.bfloat16), "seq", scatter_dimension=0, tiled=True
        ).astype(jnp.float32),
    )
    grad_key = grad_keys.astype(jnp.bfloat16)
    grad_value = grad_values.astype(jnp.bfloat16)
    grad_query = join_heads(grad_qh).astype(jnp.bfloat16)
    grad_qkv = jnp.concatenate([grad_query, grad_key, grad_value], axis=1)
    grad_tokens = grad_zone + times_transpose(grad_qkv, qkv_back)
    grad_qkvw = contract_rows(tokens, grad_qkv)
    grad_qbias = jnp.sum(grad_query.astype(jnp.float32), axis=0)
    grad_vbias = jnp.sum(grad_value.astype(jnp.float32), axis=0)
    shares = (
        lax.psum_scatter(grad_qkvw, ("fsdp", "seq"), scatter_dimension=0, tiled=True),
        lax.psum_scatter(grad_qbias, ("fsdp", "seq"), scatter_dimension=0, tiled=True),
        lax.psum_scatter(grad_vbias, ("fsdp", "seq"), scatter_dimension=0, tiled=True),
        lax.psum_scatter(grad_outw, ("fsdp", "seq"), scatter_dimension=0, tiled=True),
        lax.psum_scatter(grad_outb, ("fsdp", "seq"), scatter_dimension=0, tiled=True),
        lax.psum_scatter(grad_gain_one, ("fsdp", "seq"), scatter_dimension=0, tiled=True),
        lax.psum_scatter(grad_shift_one, ("fsdp", "seq"), scatter_dimension=0, tiled=True),
        lax.psum_scatter(grad_upw, ("fsdp", "seq"), scatter_dimension=0, tiled=True),
        lax.psum_scatter(grad_upb, ("fsdp", "seq"), scatter_dimension=0, tiled=True),
        lax.psum_scatter(grad_downw, ("fsdp", "seq"), scatter_dimension=0, tiled=True),
        lax.psum_scatter(grad_downb, ("fsdp", "seq"), scatter_dimension=0, tiled=True),
        lax.psum_scatter(grad_gain_two, ("fsdp", "seq"), scatter_dimension=0, tiled=True),
        lax.psum_scatter(grad_shift_two, ("fsdp", "seq"), scatter_dimension=0, tiled=True),
    )
    return (
        result.astype(jnp.bfloat16),
        grad_tokens,
        shares[0],
        shares[1],
        shares[2],
        shares[3],
        shares[4],
        shares[5],
        shares[6],
        shares[7],
        shares[8],
        shares[9],
        shares[10],
        shares[11],
        shares[12],
    )


def solution(mesh):
    placed = (
        P(("fsdp", "seq"), None),
        P("fsdp", None),
        P("fsdp", None),
        P(("fsdp", "seq"), None),
        P(("fsdp", "seq")),
        P(("fsdp", "seq")),
        P(("fsdp", "seq"), None),
        P(("fsdp", "seq")),
        P(("fsdp", "seq")),
        P(("fsdp", "seq")),
        P(("fsdp", "seq"), None),
        P(("fsdp", "seq")),
        P(("fsdp", "seq"), None),
        P(("fsdp", "seq")),
        P(("fsdp", "seq")),
        P(("fsdp", "seq")),
        P(("fsdp", "seq"), None),
    )
    return jax.shard_map(
        shards,
        mesh=mesh,
        in_specs=placed,
        out_specs=(
            P(("fsdp", "seq"), None),
            P(("fsdp", "seq"), None),
            P(("fsdp", "seq"), None),
            P(("fsdp", "seq")),
            P(("fsdp", "seq")),
            P(("fsdp", "seq"), None),
            P(("fsdp", "seq")),
            P(("fsdp", "seq")),
            P(("fsdp", "seq")),
            P(("fsdp", "seq"), None),
            P(("fsdp", "seq")),
            P(("fsdp", "seq"), None),
            P(("fsdp", "seq")),
            P(("fsdp", "seq")),
            P(("fsdp", "seq")),
        ),
        check_vma=False,
    )
```

profile of v0, /device:TPU:0, one launch (start us, length us, event | category | flops | bytes accessed | tf_op | source)
XLA Modules:
  0.0 2419.0 jit_solution(2322725565926865196)
XLA Ops:
  9.4 310.0 %all-gather.16.cloned.1.call-done = bf16[128,6,2304]{2,1,0:T(8,128)(2,1)} async-done(((bf16[1,6,2304]{2,1,0:T(8,128)(2,1)}), bf16[128,6,2304]{2,1,0:T(8,128)(2,1)}) %all-gather.16.cloned.1.call-update) | async-done | bytes 3538960 | tf_op jit(solution)/shard_map/all_gather | solution.py:58
  319.5 5.0 reshape.177
  338.0 67.1 %all-reduce.24 = (bf16[768]{0:T(1024)(128)(2,1)}, bf16[768]{0:T(1024)(128)(2,1)}, bf16[768]{0:T(1024)(128)(2,1)}, bf16[768]{0:T(1024)(128)(2,1)}, bf16[768]{0:T(...) all-reduce(bf16[768]{0:T(1024)(128)(2,1)S(1)} %dynamic-update-slice, ...), channel_id=1, replica_groups=mesh['fsdp'=16,'seq'=8] {'fsdp','seq'}, use_global_device_ids=true, to_apply=%add | all-reduce | flops 9216 | bytes 36864
  419.7 200.9 %all-gather.18.cloned.1.call-done = bf16[128,6,768]{2,1,0:T(8,128)(2,1)} async-done(((bf16[1,6,768]{2,1,0:T(8,128)(2,1)}), bf16[128,6,768]{2,1,0:T(8,128)(2,1)}) %all-gather.18.cloned.1.call-update) | async-done | bytes 1179664 | tf_op jit(solution)/shard_map/all_gather | solution.py:61
  620.6 3.2 reshape.179
  627.9 306.2 %all-gather.20.cloned.1.call-done = bf16[128,6,3072]{2,1,0:T(8,128)(2,1)} async-done(((bf16[1,6,3072]{2,1,0:T(8,128)(2,1)}), bf16[128,6,3072]{2,1,0:T(8,128)(2,1)}) %all-gather.20.cloned.1.call-update) | async-done | bytes 4718608 | tf_op jit(solution)/shard_map/all_gather | solution.py:65
  934.1 7.7 reshape.181
  941.8 39.8 %all-gather.10.cloned.1.call-done = bf16[2048,768]{1,0:T(8,128)(2,1)} async-done(((bf16[256,768]{1,0:T(8,128)(2,1)}), bf16[2048,768]{1,0:T(8,128)(2,1)}) %all-gather.10.cloned.1.call-update) | async-done | bytes 3145744 | tf_op jit(solution)/shard_map/all_gather | solution.py:109
  981.6 4.7 copy.62
  986.3 6.6 copy.65
  992.9 34.7 %all-gather.12.cloned.1.call-done = bf16[2048,768]{1,0:T(8,128)(2,1)} async-done(((bf16[256,768]{1,0:T(8,128)(2,1)}), bf16[2048,768]{1,0:T(8,128)(2,1)}) %all-gather.12.cloned.1.call-update) | async-done | bytes 3145744 | tf_op jit(solution)/shard_map/all_gather | solution.py:110
  1027.5 4.7 copy.63
  1032.3 6.6 copy.66
  1039.7 74.2 %while.28 = (s32[]{:T(128)}, bf16[12,256,64]{1,2,0:T(8,128)(2,1)}, f32[12,256]{1,0:T(8,128)}, bf16[12,256,64]{2,1,0:T(8,128)(2,1)}, bf16[12,2048,64]{2,1,0:T(8,1...) while((s32[]{:T(128)}, bf16[12,256,64]{1,2,0:T(8,128)(2,1)}, ...), condition=%wide.region_5.6_spmd.clone, body=%wide.region_2.5_spmd.clone.sunk | while | flops 138936064 | bytes 7492721 | solution.py:127
  1117.4 5.6 convolution_add_fusion
  1123.0 214.2 %all-gather.14.cloned.1.call-done = bf16[3072,768]{1,0:T(8,128)(2,1)} async-done(((bf16[24,768]{1,0:T(8,128)(2,1)}), bf16[3072,768]{1,0:T(8,128)(2,1)}) %all-gather.14.cloned.1.call-update) | async-done | bytes 4718608 | tf_op jit(solution)/shard_map/all_gather | solution.py:67
  1337.2 5.7 fusion.83
  1345.8 3.8 convert_reduce_fusion
  1357.6 122.0 %while.29 = (s32[]{:T(128)}, bf16[12,256,64]{1,2,0:T(8,128)(2,1)}, bf16[12,2048,64]{1,2,0:T(8,128)(2,1)}, bf16[12,2048,64]{1,2,0:T(8,128)(2,1)}, bf16[12,256,64]...) while((s32[]{:T(128)}, bf16[12,256,64]{1,2,0:T(8,128)(2,1)}, ...), condition=%wide.region_16.17_spmd.clone, body=%wide.region_14.16_spmd.clone.sunk | while | flops 340934400 | bytes 18631808 | solution.py:192
  1480.5 46.3 %reduce-scatter.11.cloned.1.call-done = bf16[256,768]{0,1:T(8,128)(2,1)} async-done(((bf16[2048,768]{0,1:T(8,128)(2,1)}), bf16[256,768]{0,1:T(8,128)(2,1)}) %reduce-scatter.11.cloned.1.call-update) | async-done | bytes 393232 | tf_op jit(solution)/shard_map/reduce_scatter | solution.py:199
  1526.8 48.3 %reduce-scatter.9.cloned.1.call-done = bf16[256,768]{0,1:T(8,128)(2,1)} async-done(((bf16[2048,768]{0,1:T(8,128)(2,1)}), bf16[256,768]{0,1:T(8,128)(2,1)}) %reduce-scatter.9.cloned.1.call-update) | async-done | bytes 393232 | tf_op jit(solution)/shard_map/reduce_scatter | solution.py:196
  1575.1 5.4 convolution_bitcast_fusion.2
  1580.5 8.0 fusion.70
  1588.6 3.4 fusion.67
  1592.0 5.2 fusion.76
  1597.2 386.9 %fusion.79 = (f32[8,768]{1,0:T(8,128)}, f32[8,3072]{1,0:T(8,128)}) fusion(f32[768,768]{1,0:T(8,128)} %fusion.67, f32[768,3072]{1,0:T(8,128)} %fusion.76), kind=kCustom, calls=%all-reduce-scatter.2 | all-reduce-scatter fusion | flops 3932161 | bytes 11919360
  1996.8 19.1 collective-permute-start.22
  2016.0 3.2 collective-permute-start.21
  2019.2 3.4 collective-permute-start.20
  2032.1 6.5 collective-permute-start.14
  2043.0 5.0 collective-permute-start.10
  2056.0 5.4 collective-permute-start.6
  2071.5 4.0 collective-permute-start.2
  2075.5 3.7 collective-permute-start.1
  2095.6 3.3 collective-permute-start.55
  2101.6 4.0 collective-permute-start.53
  2114.2 4.6 collective-permute-start.49
  2122.7 4.5 collective-permute-start.46
  2134.4 6.2 collective-permute-start.42
  2140.6 5.5 collective-permute-start.41
  2149.9 3.3 collective-permute-start.38
  2158.0 47.1 %concatenate.4 = f32[262,768]{1,0:T(8,128)} concatenate(f32[6,768]{1,0:T(8,128)} %copy-done.19, f32[8,768]{1,0:T(8,128)} %copy-done.16, f32[8,768]{1,0:T(8,128)} %copy-done.17, f32[8,768]{1,0:T(8,128)} %copy-done.18, f32[8,768]{1,0:T(8,128)} %copy-done.20, f32[8,768]{1,0:T(8,128)} %copy-done.21, f32[8,768]{1,0:T(8,128)} %copy-done.22, f32[8,768]{1,0:T(8,128)} %copy-done.23, ...), dimensions={0} | concatenate | bytes 1609728
  2209.8 4.3 collective-permute-start.34
  2214.1 3.4 collective-permute-start.33
  2221.4 55.9 %concatenate.5 = f32[262,3072]{1,0:T(8,128)} concatenate(f32[6,3072]{1,0:T(8,128)} %copy-done.11, f32[8,3072]{1,0:T(8,128)} %collective-permute-done.62, f32[8,3072]{1,0:T(8,128)} %collective-permute-done.61, f32[8,3072]{1,0:T(8,128)} %collective-permute-done.60, f32[8,3072]{1,0:T(8,128)} %collective-permute-done.59, f32[8,3072]{1,0:T(8,128)} %collective-permute-done.58, ...), dimensions={0} | concatenate | bytes 6438912
  2280.7 66.4 %all-reduce.23 = (f32[768]{0:T(1024)}, f32[768]{0:T(1024)}, f32[768]{0:T(1024)}, f32[768]{0:T(1024)}, f32[768]{0:T(1024)}, /*index=5*/f32[3072]{0:T(1024)}, f32[768]{0:T(1024)}, f32[768]{0:T(1024)}, f32[768]{0:T(1024)}) all-reduce(f32[768]{0:T(1024)} %reduce_sum.192, ...), channel_id=5, replica_groups=mesh['fsdp'=16,'seq'=8] {'fsdp','seq'}, use_global_device_ids=true, to_apply=%region_21.22.clone | all-reduce | flops 9216 | bytes 73728
  2358.5 3.5 convolution_add_fusion.2
  2365.0 46.7 %reduce-scatter.13.cloned.1.call-done = f32[24,768]{1,0:T(8,128)} async-done(((f32[3072,768]{1,0:T(8,128)}), f32[24,768]{1,0:T(8,128)}) %reduce-scatter.13.cloned.1.call-update) | async-done | bytes 73744 | tf_op jit(solution)/shard_map/reduce_scatter | solution.py:221
  (484 shorter events, 364.0 us)
Async XLA Ops:
  7.2 312.3 %all-gather.16.cloned.1.call-start = ((), (), s32[]{:S(2)}) async-start(), calls=%async_computation.9 | async-start | bytes 4755456 | tf_op jit(solution)/shard_map/all_gather | solution.py:58
  7.9 612.6 %all-gather.18.cloned.1.call-start = ((), (), s32[]{:S(2)}) async-start(), calls=%async_computation.10 | async-start | bytes 1585152 | tf_op jit(solution)/shard_map/all_gather | solution.py:61
  8.7 925.4 %all-gather.20.cloned.1.call-start = ((), (), s32[]{:S(2)}) async-start(), calls=%async_computation.11 | async-start | bytes 6340608 | tf_op jit(solution)/shard_map/all_gather | solution.py:65
  9.4 972.2 %all-gather.10.cloned.1.call-start = ((), (), s32[]{:S(2)}) async-start(), calls=%async_computation.3 | async-start | bytes 3538944 | tf_op jit(solution)/shard_map/all_gather | solution.py:109
  328.9 698.6 %all-gather.12.cloned.1.call-start = ((), (), s32[]{:S(2)}) async-start(), calls=%async_computation.4 | async-start | bytes 3538944 | tf_op jit(solution)/shard_map/all_gather | solution.py:110
  408.9 928.2 %all-gather.14.cloned.1.call-start = ((), (), s32[]{:S(2)}) async-start(), calls=%async_computation.5 | async-start | bytes 4755456 | tf_op jit(solution)/shard_map/all_gather | solution.py:67
  409.5 1117.3 %reduce-scatter.11.cloned.1.call-start = ((), (), s32[]{:S(2)}) async-start(), calls=%async_computation.7 | async-start | bytes 3538944 | tf_op jit(solution)/shard_map/reduce_scatter | solution.py:199
  1479.7 95.4 %reduce-scatter.9.cloned.1.call-start = ((), (), s32[]{:S(2)}) async-start(), calls=%async_computation.6 | async-start | bytes 3538944 | tf_op jit(solution)/shard_map/reduce_scatter | solution.py:196
  1480.4 881.6 %all-reduce.28.cloned.1.call-start = ((), (), s32[]{:S(2)}) async-start(), calls=%async_computation.12 | async-start | bytes 14155776
  1580.4 831.2 %reduce-scatter.13.cloned.1.call-start = ((), (), s32[]{:S(2)}) async-start(), calls=%async_computation.8 | async-start | bytes 9510912 | tf_op jit(solution)/shard_map/reduce_scatter | solution.py:221
  1991.5 24.4 %collective-permute-start.26 = (f32[8,768]{1,0:T(8,128)}, f32[8,768]{1,0:T(8,128)S(1)}, u32[]{:S(2)}, u32[]{:S(2)}) collective-permute-start(f32[8,768]{1,0:T(8,128)} %get-tuple-element.341), channel_id=1, source_target_pairs={{0,27},{1,28},{2,29},{3,30},{4,31},{5,32},{6,33},{7,34},{8,35},{9,... | collective-permute-start | bytes 73736
  1992.8 26.4 %collective-permute-start.25 = (f32[8,768]{1,0:T(8,128)}, f32[8,768]{1,0:T(8,128)S(1)}, u32[]{:S(2)}, u32[]{:S(2)}) collective-permute-start(f32[8,768]{1,0:T(8,128)} %get-tuple-element.341), channel_id=1, source_target_pairs={{0,26},{1,27},{2,28},{3,29},{4,30},{5,31},{6,32},{7,33},{8,34},{9,... | collective-permute-start | bytes 73736
  1994.1 28.5 %collective-permute-start.24 = (f32[8,768]{1,0:T(8,128)}, f32[8,768]{1,0:T(8,128)S(1)}, u32[]{:S(2)}, u32[]{:S(2)}) collective-permute-start(f32[8,768]{1,0:T(8,128)} %get-tuple-element.341), channel_id=1, source_target_pairs={{0,25},{1,26},{2,27},{3,28},{4,29},{5,30},{6,31},{7,32},{8,33},{9,... | collective-permute-start | bytes 73736
  1995.5 28.5 %collective-permute-start.23 = (f32[8,768]{1,0:T(8,128)}, f32[8,768]{1,0:T(8,128)S(1)}, u32[]{:S(2)}, u32[]{:S(2)}) collective-permute-start(f32[8,768]{1,0:T(8,128)} %get-tuple-element.341), channel_id=1, source_target_pairs={{0,24},{1,25},{2,26},{3,27},{4,28},{5,29},{6,30},{7,31},{8,32},{9,... | collective-permute-start | bytes 73736
  1996.8 29.4 %collective-permute-start.22 = (f32[8,768]{1,0:T(8,128)}, f32[8,768]{1,0:T(8,128)S(1)}, u32[]{:S(2)}, u32[]{:S(2)}) collective-permute-start(f32[8,768]{1,0:T(8,128)} %get-tuple-element.341), channel_id=1, source_target_pairs={{0,23},{1,24},{2,25},{3,26},{4,27},{5,28},{6,29},{7,30},{8,31},{9,... | collective-permute-start | bytes 73736
  2024.0 14.6 collective-permute-start.18
  2026.2 13.9 collective-permute-start.17
  2027.6 13.9 collective-permute-start.16
  2030.3 12.8 collective-permute-start.15
  2032.1 15.9 collective-permute-start.14
  2048.1 14.3 collective-permute-start.9
  2050.4 41.3 %collective-permute-start.62 = (f32[8,3072]{1,0:T(8,128)}, f32[8,3072]{1,0:T(8,128)}, u32[]{:S(2)}, u32[]{:S(2)}) collective-permute-start(f32[8,3072]{1,0:T(8,128)} %get-tuple-element.342), channel_id=1, source_target_pairs={{0,31},{1,32},{2,33},{3,34},{4,35},{5,36},{6,37},{7,38},{8,39},{9,... | collective-permute-start | bytes 294920
  2053.8 12.9 collective-permute-start.7
  2056.0 12.9 collective-permute-start.6
  2062.4 26.8 %collective-permute-start.63 = (f32[6,3072]{1,0:T(8,128)S(1)}, f32[6,3072]{1,0:T(8,128)S(1)}, u32[]{:S(2)}, u32[]{:S(2)}) collective-permute-start(f32[6,3072]{1,0:T(8,128)S(1)} %slice.17), channel_id=1, source_target_pairs={{0,32},{1,33},{2,34},{3,35},{4,36},{5,37},{6,38},{7,39},{8,40},{9,... | collective-permute-start | bytes 221192
  2091.7 13.9 collective-permute-start.57
  2093.7 14.8 collective-permute-start.56
  2095.6 15.5 collective-permute-start.55
  2098.9 15.3 collective-permute-start.54
  2101.6 17.1 collective-permute-start.53
  2105.6 15.1 collective-permute-start.52
  2108.5 14.2 collective-permute-start.51
  2111.1 16.2 collective-permute-start.50
  2114.2 15.8 collective-permute-start.49
  2118.7 13.2 collective-permute-start.48
  2120.8 13.6 collective-permute-start.47
  2122.7 17.9 collective-permute-start.46
  2127.2 18.8 collective-permute-start.45
  2130.0 18.0 collective-permute-start.44
  2131.9 18.0 collective-permute-start.43
  2134.4 18.8 collective-permute-start.42
  2140.6 64.5 %collective-permute-start.41 = (f32[8,3072]{1,0:T(8,128)}, f32[8,3072]{1,0:T(8,128)}, u32[]{:S(2)}, u32[]{:S(2)}) collective-permute-start(f32[8,3072]{1,0:T(8,128)} %get-tuple-element.342), channel_id=1, source_target_pairs={{0,10},{1,11},{2,12},{3,13},{4,14},{5,15},{6,16},{7,17},{8,18},{9,... | collective-permute-start | bytes 294920
  2146.1 61.8 %collective-permute-start.40 = (f32[8,3072]{1,0:T(8,128)}, f32[8,3072]{1,0:T(8,128)}, u32[]{:S(2)}, u32[]{:S(2)}) collective-permute-start(f32[8,3072]{1,0:T(8,128)} %get-tuple-element.342), channel_id=1, source_target_pairs={{0,9},{1,10},{2,11},{3,12},{4,13},{5,14},{6,15},{7,16},{8,17},{9,1... | collective-permute-start | bytes 294920
  2148.0 61.8 %collective-permute-start.39 = (f32[8,3072]{1,0:T(8,128)}, f32[8,3072]{1,0:T(8,128)}, u32[]{:S(2)}, u32[]{:S(2)}) collective-permute-start(f32[8,3072]{1,0:T(8,128)} %get-tuple-element.342), channel_id=1, source_target_pairs={{0,8},{1,9},{2,10},{3,11},{4,12},{5,13},{6,14},{7,15},{8,16},{9,17... | collective-permute-start | bytes 294920
  2149.9 64.2 %collective-permute-start.38 = (f32[8,3072]{1,0:T(8,128)}, f32[8,3072]{1,0:T(8,128)}, u32[]{:S(2)}, u32[]{:S(2)}) collective-permute-start(f32[8,3072]{1,0:T(8,128)} %get-tuple-element.342), channel_id=1, source_target_pairs={{0,7},{1,8},{2,9},{3,10},{4,11},{5,12},{6,13},{7,14},{8,15},{9,16}... | collective-permute-start | bytes 294920
  2153.2 64.3 %collective-permute-start.37 = (f32[8,3072]{1,0:T(8,128)}, f32[8,3072]{1,0:T(8,128)}, u32[]{:S(2)}, u32[]{:S(2)}) collective-permute-start(f32[8,3072]{1,0:T(8,128)} %get-tuple-element.342), channel_id=1, source_target_pairs={{0,6},{1,7},{2,8},{3,9},{4,10},{5,11},{6,12},{7,13},{8,14},{9,15},... | collective-permute-start | bytes 294920
  2205.0 15.8 collective-permute-start.36
  2207.9 13.0 collective-permute-start.35
  (92 other events, 1453.8 us)
Sparse Core Ops, SparseCore 0:
  9.7 309.7 all-gather.15
  321.2 299.3 all-gather.17
  622.3 311.7 all-gather.19
  935.6 45.9 all-gather.9
  983.6 43.8 all-gather.11
  1029.1 308.0 all-gather.13
  1479.8 46.9 reduce-scatter.10
  1529.2 45.8 reduce-scatter.8
  1580.6 167.3 all-reduce.27
  1750.9 660.7 reduce-scatter.12
where the time goes:
time: 2430 us; the launch traced here: 2420 us
  waiting for transfers between devices  1250 us (51%)
  blocking collectives  520 us (21%)
  local copies, waits for them, and re-layouts  209 us (9%)
  matrix products  205 us (8%)
  starting transfers between devices  183 us (8%)
  other arithmetic  35 us (1%)
    unnamed x3, blocking collectives  520 us
    all_gather x1, waiting for transfers between devices, shards(): lax.all_gather(qkv_weight, ('fsdp', 'seq'), axis=0, tiled=True)  310 us
    all_gather x1, waiting for transfers between devices, shards(): lax.all_gather(up_weight, ('fsdp', 'seq'), axis=0, tiled=True)  306 us
    all_gather x1, waiting for transfers between devices, shards(): lax.all_gather(down_weight, ('fsdp', 'seq'), axis=0, tiled=True)  214 us
    all_gather x1, waiting for transfers between devices, shards(): lax.all_gather(out_weight, ('fsdp', 'seq'), axis=0, tiled=True)  201 us
    unnamed x65, starting transfers between devices  182 us
    unnamed x173, local copies, waits for them, and re-layouts  167 us
  transfers between devices with their start and end apart: 74, of which 11 were waited for; matrix products, arithmetic and copies ran while one was open for 28% of the time, Pallas kernels for 0%

commit v1 on v0

v1 whole, which is shorter than its diff:
```python
import functools

import jax
import jax.numpy as jnp
from jax import lax
from jax.experimental import pallas as pl
from jax.experimental.pallas import tpu as pltpu
from jax.sharding import PartitionSpec as P

MESH = pl.DeviceIdType.MESH
BF, F32 = jnp.bfloat16, jnp.float32
EPS = 1e-12
D, FF, T = 768, 3072, 256
NA, NB, NC = 2432, 3968, 896
WIDE = ((24, NA), (24, NB), (96, NC))
TALL = ((16, NA), (16, NB), (32, NC))
ROWS = (6, 6, 24)
ROUTES = (
    ("yz", (((0, 0, NA),), ((2, 0, 640),))),
    ("zy", (((2, 640, 256), (1, 0, 1408)), ((1, 1408, 2560),))),
)
CHUNKS = (((0, 0, NA), (2, 0, 640)), ((2, 640, 256), (1, 0, NB)))
BOTH = (0, 1)


def coords():
    f, s = lax.axis_index("fsdp"), lax.axis_index("seq")
    return s % 4, (f // 2) % 4, (f // 8) * 2 + s // 4, f % 2


def ident(x, y, z, core):
    return {"fsdp": (z // 2) * 8 + y * 2 + core, "seq": (z % 2) * 4 + x}


def block_of(y, z, core):
    return (z // 2) * 16 + y * 4 + core * 2 + z % 2


def greet(partners):
    barrier = pltpu.get_barrier_semaphore()
    for who in partners:
        pl.semaphore_signal(barrier, inc=1, device_id=who, device_id_type=MESH)
    pl.semaphore_wait(barrier, len(partners))


def remote(src, dst, send, recv, who):
    return pltpu.make_async_remote_copy(
        src, dst, send, recv, device_id=who, device_id_type=MESH
    )


def dot(a, b):
    return jnp.dot(a, b, preferred_element_type=F32)


def dot_t(a, b):
    return lax.dot_general(a, b, (((1,), (1,)), ((), ())), preferred_element_type=F32)


def dot_rows(a, b):
    return lax.dot_general(a, b, (((0,), (0,)), ((), ())), preferred_element_type=F32)


def picker(shape, rows, at, transposed):
    i = lax.broadcasted_iota(jnp.int32, shape, 0)
    j = lax.broadcasted_iota(jnp.int32, shape, 1)
    if transposed:
        i, j = j, i
    return jnp.where((i == at * rows + j) & (j < rows), 1.0, 0.0).astype(BF)


def neighbours(x, y, z, core):
    peers = [ident((x + d) % 4, y, z, core) for d in (1, 2, 3)]
    rings = {
        "y": [ident(x, (y + d) % 4, z, core) for d in (1, 3)],
        "z": [ident(x, y, (z + d) % 4, core) for d in (1, 3)],
    }
    return peers, rings, ident(x, y, z, 1 - core)


def across(x, y, z, core):
    other = z + 1 - 2 * (z % 2)
    return [ident((x + d) % 4, y, other, core) for d in range(4)]


def gather_kernel(
    s0, s1, s2, tokens, w0, w1, w2, q_out, kv_out,
    x0, x1, x2, own0, own1, own2, land, q_land, kv_land, q_slab, kv_slab,
    x_send, x_recv, put_sem, send, recv, core_send, core_recv, q_send, q_recv, kv_send, kv_recv,
):
    x, y, z, core = coords()
    slabs, arrived, own = (s0, s1, s2), (x0, x1, x2), (own0, own1, own2)
    wide = (land, w1, w2)
    peers, rings, sibling = neighbours(x, y, z, core)
    others = across(x, y, z, core)
    greet(peers + rings["y"] + rings["z"] + [sibling] + others)
    x_copies = []
    for d in (1, 3, 2):
        for k in range(3):
            c = remote(slabs[k], arrived[k].at[d - 1], x_send.at[d - 1, k], x_recv.at[d - 1, k], peers[d - 1])
            c.start()
            x_copies.append(c)
    for c in x_copies:
        c.wait_recv()
    for k, rows in enumerate(ROWS):
        shape = (4 * rows, TALL[k][0])
        total = jnp.zeros(WIDE[k], F32)
        for d in range(4):
            slab = slabs[k][...] if d == 0 else arrived[k][d - 1]
            total += dot(picker(shape, rows, (x + 4 - d) % 4, False), slab)
        own[k][...] = total.astype(BF)

    me = block_of(y, z, core)
    puts = [pltpu.make_async_copy(own[k], wide[k].at[me], put_sem.at[k]) for k in range(3)]
    for c in puts:
        c.start()
    started, shared = [], []

    def place(route, a, b, c):
        dy, dz = (a, b) if ROUTES[route][0] == "yz" else (b, a)
        return block_of((y + dy) % 4, (z + dz) % 4, c)

    def source(k, route, a, b):
        return own[k] if a == 0 and b == 0 else wide[k].at[place(route, a, b, core)]

    def push(route, i, a, b, who, sem):
        at = place(route, a, b, core)
        for j, (k, first, cols) in enumerate(ROUTES[route][1][i]):
            view = pl.ds(first, cols)
            c = remote(source(k, route, a, b).at[:, view], wide[k].at[at, :, view], send.at[sem + j], recv.at[sem + j], who)
            c.start()
            started.append(c)

    def arrive(route, i, a, b, sem):
        for j, (k, first, cols) in enumerate(ROUTES[route][1][i]):
            view = wide[k].at[place(route, a, b, core), :, pl.ds(first, cols)]
            remote(view, view, send.at[sem + j], recv.at[sem + j], sibling).wait_recv()

    def share(route, a, b):
        at = place(route, a, b, core)
        for k, first, cols in CHUNKS[route]:
            n, view = len(shared), pl.ds(first, cols)
            c = remote(source(k, route, a, b).at[:, view], wide[k].at[at, :, view], core_send.at[n], core_recv.at[n], sibling)
            c.start()
            shared.append((c, route, a, b, k, view))

    def slot(route, group, kind, i):
        return (route * 5 + group) * 9 + kind * 3 + (len(ROUTES[route][1][0]) if i else 0)

    def axis(route, group):
        return rings[ROUTES[route][0][0 if group == 0 else 1]]

    def begin(route, group, a, b):
        for turn in BOTH:
            for i in BOTH:
                push(route, i, a, b, axis(route, group)[turn], slot(route, group, turn, i))

    def onward(route, group, turn, a, b):
        for i in BOTH:
            arrive(route, i, a, b, slot(route, group, turn, i))
        push(route, turn, a, b, axis(route, group)[turn], slot(route, group, 2, turn))

    def finish(route, group, a, b):
        for i in BOTH:
            arrive(route, i, a, b, slot(route, group, 2, i))

    for r in BOTH:
        begin(r, 0, 0, 0)
    for r in BOTH:
        begin(r, 1, 0, 0)
    for r in BOTH:
        share(r, 0, 0)
    for turn, a in ((0, 3), (1, 1)):
        for r in BOTH:
            onward(r, 0, turn, a, 0)
            begin(r, 1 + a, a, 0)
            share(r, a, 0)
    for turn, b in ((0, 3), (1, 1)):
        for r in BOTH:
            onward(r, 1, turn, 0, b)
            share(r, 0, b)
    for r in BOTH:
        finish(r, 0, 2, 0)
        begin(r, 3, 2, 0)
        share(r, 2, 0)
    for a in (3, 1):
        for turn, b in ((0, 3), (1, 1)):
            for r in BOTH:
                onward(r, 1 + a, turn, a, b)
                share(r, a, b)
    for r in BOTH:
        finish(r, 1, 0, 2)
        share(r, 0, 2)
    for turn, b in ((0, 3), (1, 1)):
        for r in BOTH:
            onward(r, 3, turn, 2, b)
            share(r, 2, b)
    for a in (3, 1, 2):
        for r in BOTH:
            finish(r, 1 + a, a, 2)
            share(r, a, 2)
    for n, (c, route, a, b, k, view) in enumerate(shared):
        got = wide[k].at[place(route, a, b, 1 - core), :, view]
        remote(got, got, core_send.at[n], core_recv.at[n], sibling).wait_recv()
        c.wait_send()
    for c in x_copies + started:
        c.wait_send()
    for c in puts:
        c.wait()

    keep = pltpu.make_async_copy(land, w0, put_sem.at[0])
    keep.start()
    weight = land[...].reshape(D, NA)
    biases = weight[:, 3 * D :].astype(F32).T
    qkv = dot(tokens[...], weight[:, : 3 * D])
    query = (qkv[:, :D] + biases[0:1]).astype(BF).astype(F32) * 0.125
    key = qkv[:, D : 2 * D]
    value = qkv[:, 2 * D :] + biases[1:2]
    for g in range(4):
        at = g * 192
        q_slab[g] = jnp.concatenate(
            [query[:, at : at + 192], jnp.zeros((T, 64), F32)], axis=1
        ).astype(BF)
        kv_slab[g] = jnp.concatenate(
            [key[:, at : at + 128], value[:, at : at + 128], key[:, at + 128 : at + 192], value[:, at + 128 : at + 192]], axis=1
        ).astype(BF)
    mine = (z % 2) * 4 + x
    copies = []
    for d in range(4):
        to = (x + d) % 4
        c = remote(kv_slab.at[to], kv_land.at[mine], kv_send.at[4 + d], kv_recv.at[4 + d], others[d])
        c.start()
        copies.append((c, kv_land.at[(1 - z % 2) * 4 + (x + 4 - d) % 4], kv_send.at[4 + d], kv_recv.at[4 + d]))
    for d in (2, 1, 3):
        to, fro = (x + d) % 4, (x + 4 - d) % 4
        for slab, landing, place_to, place_from, ss, rr in (
            (kv_slab, kv_land, mine, (z % 2) * 4 + fro, kv_send, kv_recv),
            (q_slab, q_land, x, fro, q_send, q_recv),
        ):
            c = remote(slab.at[to], landing.at[place_to], ss.at[d], rr.at[d], peers[d - 1])
            c.start()
            copies.append((c, landing.at[place_from], ss.at[d], rr.at[d]))
    kv_land[mine] = kv_slab[x]
    q_land[x] = q_slab[x]
    for c, got, ss, rr in copies:
        remote(got, got, ss, rr, sibling).wait_recv()
    for c, got, ss, rr in copies:
        c.wait_send()
    outs = [pltpu.make_async_copy(q_land, q_out, put_sem.at[1]), pltpu.make_async_copy(kv_land, kv_out, put_sem.at[2])]
    for c in outs:
        c.start()
    for c in outs + [keep]:
        c.wait()


ANY = pl.BlockSpec(memory_space=pl.ANY)
VM = pl.BlockSpec(memory_space=pltpu.VMEM)
DMA = pltpu.SemaphoreType.DMA


def struct(shape, kind):
    return jax.ShapeDtypeStruct(shape, kind)


def gather_weights(s0, s1, s2, tokens):
    return pl.pallas_call(
        gather_kernel,
        out_shape=tuple(struct((32,) + w, BF) for w in WIDE) + (struct((4, T, 256), BF), struct((8, T, 384), BF)),
        in_specs=[VM] * 4,
        out_specs=(ANY,) * 5,
        scratch_shapes=[pltpu.VMEM((3,) + t, BF) for t in TALL]
        + [pltpu.VMEM(w, BF) for w in WIDE]
        + [pltpu.VMEM((32,) + WIDE[0], BF), pltpu.VMEM((4, T, 256), BF), pltpu.VMEM((8, T, 384), BF)]
        + [pltpu.VMEM((4, T, 256), BF), pltpu.VMEM((4, T, 384), BF)]
        + [DMA((3, 3)), DMA((3, 3)), DMA((3,)), DMA((90,)), DMA((90,)), DMA((64,)), DMA((64,))]
        + [DMA((4,)), DMA((4,)), DMA((8,)), DMA((8,))],
        compiler_params=pltpu.CompilerParams(collective_id=0, has_side_effects=True, vmem_limit_bytes=48 << 20),
        name="gather_weights",
    )(s0, s1, s2, tokens)


def head_lanes(tile, h):
    lane = lax.broadcasted_iota(jnp.int32, (1, 128), 1)
    return (lane < 64) if h % 2 == 0 else (lane >= 64)


def attend_kernel(q_ref, kv_ref, qseg, kseg, o_ref, lse_ref):
    allowed = qseg[:, :1] == kseg[0:1, :]
    outs, logs = [], []
    for h in range(3):
        tile = h // 2
        lanes = head_lanes(tile, h)
        q = q_ref[:, tile * 128 : tile * 128 + 128]
        q = jnp.where(lanes, q.astype(F32), 0.0).astype(BF)
        k = kv_ref[:, 0:128] if tile == 0 else kv_ref[:, 256:384]
        v = kv_ref[:, 128:256] if tile == 0 else kv_ref[:, 256:384]
        s = jnp.where(allowed, dot_t(q, k), -1e30)
        top = jnp.max(s, axis=1, keepdims=True)
        e = jnp.exp(s - top)
        total = jnp.sum(e, axis=1, keepdims=True)
        outs.append(dot(e.astype(BF), v) / total)
        logs.append(top + jnp.log(total))
    first = head_lanes(0, 0)
    o_ref[:, 0:128] = jnp.where(first, outs[0], outs[1]).astype(BF)
    o_ref[:, 128:256] = jnp.where(first, 0.0, outs[2]).astype(BF)
    lane = lax.broadcasted_iota(jnp.int32, (1, 128), 1)
    lse_ref[...] = jnp.where(lane == 0, logs[0], jnp.where(lane == 1, logs[1], logs[2]))


def attend(q, kv, qseg, kseg):
    step = 256
    return pl.pallas_call(
        attend_kernel,
        grid=(1024 // step,),
        out_shape=(struct((1024, 256), BF), struct((1024, 128), F32)),
        in_specs=[
            pl.BlockSpec((step, 256), lambda i: (i, 0)),
            pl.BlockSpec((2048, 384), lambda i: (0, 0)),
            pl.BlockSpec((step, 128), lambda i: (i, 0)),
            pl.BlockSpec((8, 2048), lambda i: (0, 0)),
        ],
        out_specs=(pl.BlockSpec((step, 256), lambda i: (i, 0)), pl.BlockSpec((step, 128), lambda i: (i, 0))),
        compiler_params=pltpu.CompilerParams(vmem_limit_bytes=48 << 20),
        name="attend",
    )(q, kv, qseg, kseg)


def attend_back_kernel(q_ref, kv_ref, do_ref, o_ref, lse_ref, qseg, kseg, dq_ref, dkv_ref, total):
    step = pl.program_id(0)

    @pl.when(step == 0)
    def _():
        total[...] = jnp.zeros_like(total)

    allowed = kseg[:, :1] == qseg[0:1, :]
    logs = lse_ref[...].T
    first = head_lanes(0, 0)
    grads = []
    for h in range(3):
        tile = h // 2
        lanes = head_lanes(tile, h)
        out_lanes = lanes if h < 2 else jnp.logical_not(lanes)
        cols = slice(tile * 128, tile * 128 + 128)
        q = jnp.where(lanes, q_ref[:, cols].astype(F32), 0.0).astype(BF)
        do = jnp.where(out_lanes, do_ref[:, cols].astype(F32), 0.0)
        inner = jnp.sum(do * o_ref[:, cols].astype(F32), axis=1, keepdims=True)
        inner = jnp.broadcast_to(inner, (inner.shape[0], 128)).T[0:1]
        do = do.astype(BF)
        k = kv_ref[:, 0:128] if tile == 0 else kv_ref[:, 256:384]
        v = kv_ref[:, 128:256] if tile == 0 else kv_ref[:, 256:384]
        s = dot_t(k, q)
        p = jnp.where(allowed, jnp.exp(s - logs[h : h + 1]), 0.0)
        ds = (p * (dot_t(v, do) - inner)).astype(BF)
        dk, dv = dot(ds, q), dot(p.astype(BF), do)
        if tile == 0:
            total[:, 0:128] += dk
            total[:, 128:256] += dv
        else:
            total[:, 256:384] += dk + dv
        grads.append(dot_rows(ds, k) * 0.125)
    dq_ref[:, 0:128] = jnp.where(first, grads[0], grads[1]).astype(BF)
    dq_ref[:, 128:256] = jnp.where(first, grads[2], 0.0).astype(BF)

    @pl.when(step == pl.num_programs(0) - 1)
    def _():
        dkv_ref[...] = total[...].astype(BF)


def attend_back(q, kv, do, o, lse, qseg, kseg):
    step = 256
    rows = lambda i: (i, 0)
    return pl.pallas_call(
        attend_back_kernel,
        grid=(1024 // step,),
        out_shape=(struct((1024, 256), BF), struct((2048, 384), BF)),
        in_specs=[
            pl.BlockSpec((step, 256), rows),
            pl.BlockSpec((2048, 384), lambda i: (0, 0)),
            pl.BlockSpec((step, 256), rows),
            pl.BlockSpec((step, 256), rows),
            pl.BlockSpec((step, 128), rows),
            pl.BlockSpec((8, step), lambda i: (0, i)),
            pl.BlockSpec((2048, 128), lambda i: (0, 0)),
        ],
        out_specs=(pl.BlockSpec((step, 256), rows), pl.BlockSpec((2048, 384), lambda i: (0, 0))),
        scratch_shapes=[pltpu.VMEM((2048, 384), F32)],
        compiler_params=pltpu.CompilerParams(vmem_limit_bytes=56 << 20),
        name="attend_back",
    )(q, kv, do, o, lse, qseg, kseg)


def normalize(v):
    centered = v - jnp.mean(v, axis=-1, keepdims=True)
    factor = lax.rsqrt(jnp.mean(centered * centered, axis=-1, keepdims=True) + EPS)
    return centered * factor, factor


def norm_back(grad, normed, factor, gain):
    scaled = grad * gain
    inner = jnp.mean(scaled * normed, axis=-1, keepdims=True)
    return factor * (scaled - jnp.mean(scaled, axis=-1, keepdims=True) - normed * inner)


def middle_kernel(
    o_ref, tokens, cotangent, w1, w2, result, dz1_ref, do_out, g1, g2,
    land, do_slab, wb, wc, ext, act, slope, load, o_send, o_recv, d_send, d_recv,
):
    x, y, z, core = coords()
    peers, _, sibling = neighbours(x, y, z, core)
    loads = [pltpu.make_async_copy(w1, wb, load.at[0]), pltpu.make_async_copy(w2, wc, load.at[1])]
    for c in loads:
        c.start()
    greet(peers)

    def swap(slab, landing, ss, rr):
        copies = []
        for d in (2, 1, 3):
            c = remote(slab.at[(x + d) % 4], landing.at[x], ss.at[d - 1], rr.at[d - 1], peers[d - 1])
            c.start()
            copies.append((c, landing.at[(x + 4 - d) % 4], ss.at[d - 1], rr.at[d - 1]))
        landing[x] = slab[x]
        return copies

    copies = swap(o_ref, land, o_send, o_recv)
    for c in loads:
        c.wait()
    vectors = wb[:, :, 3840:].reshape(D, 128).astype(F32).T
    out_bias, gain_one, shift_one, down_bias, gain_two, shift_two = (vectors[i : i + 1] for i in range(6))
    for g in range(4):
        part = wb[g * 8 : g * 8 + 8, :, 0:D].reshape(192, D)
        ext[g, 0:128] = part[0:128]
        ext[g, 128:192] = jnp.zeros((64, D), BF)
        ext[g, 192:256] = part[128:192]
    for c, got, ss, rr in copies:
        remote(got, got, ss, rr, sibling).wait_recv()
        c.wait_send()
    branch = dot(land[0], ext[0])
    for g in range(1, 4):
        branch += dot(land[g], ext[g])
    normed_one, factor_one = normalize(tokens[...].astype(F32) + (branch + out_bias))
    hidden = normed_one * gain_one + shift_one
    low = hidden.astype(BF)
    feed = jnp.zeros((T, D), F32)
    for n in range(4):
        up = wb[:, :, D + n * D : 2 * D + n * D].reshape(D, D)
        down = wc[n * 8 : n * 8 + 8].reshape(D, NC)
        upper = dot(low, up) + down[:, D:].astype(F32).T[0:1]
        square = upper * upper
        t = jnp.tanh(0.7978845608028654 * (upper + 0.044715 * (square * upper)))
        half = 0.5 * (1.0 + t)
        slope[n] = half + 0.5 * upper * (1.0 - t * t) * (0.7978845608028654 * (1.0 + 3.0 * 0.044715 * square))
        act[n] = (upper * half).astype(BF)
        feed += dot(act[n], down[:, :D])
    normed_two, factor_two = normalize(hidden + (feed + down_bias))
    result[...] = (normed_two * gain_two + shift_two).astype(BF)
    grad = cotangent[...].astype(F32)
    dz2 = norm_back(grad, normed_two, factor_two, gain_two)

    def columns(v):
        return jnp.sum(v, axis=0, keepdims=True)

    gain_two_grad, shift_two_grad = columns(grad * normed_two), columns(grad)
    dfeed = dz2.astype(BF)
    down_bias_grad = columns(dfeed.astype(F32))
    dhidden = dz2

    def as_columns(rows):
        wide = [jnp.zeros((128 - len(rows), D), F32)]
        return jnp.concatenate(rows + wide, axis=0).T.astype(BF)

    for n in range(4):
        up = wb[:, :, D + n * D : 2 * D + n * D].reshape(D, D)
        down = wc[n * 8 : n * 8 + 8, :, :D].reshape(D, D)
        dupper = dot_t(dfeed, down) * slope[n]
        low_dupper = dupper.astype(BF)
        g2[n * 8 : n * 8 + 8, :, :D] = dot_rows(act[n], dfeed).astype(BF).reshape(8, 96, D)
        g2[n * 8 : n * 8 + 8, :, D:] = as_columns([columns(low_dupper.astype(F32))]).reshape(8, 96, 128)
        g1[:, :, D + n * D : 2 * D + n * D] = dot_rows(low, low_dupper).astype(BF).reshape(32, 24, D)
        dhidden += dot_t(low_dupper, up)
    dz1 = norm_back(dhidden, normed_one, factor_one, gain_one)
    dz1_ref[...] = dz1
    dbranch = dz1.astype(BF)
    for g in range(4):
        do_slab[g] = dot_t(dbranch, ext[g]).astype(BF)
    copies = swap(do_slab, do_out, d_send, d_recv)
    for g in range(4):
        part = dot_rows(land[g], dbranch).astype(BF)
        g1[g * 8 : g * 8 + 8, :, 0:D] = jnp.concatenate([part[0:128], part[192:256]], axis=0).reshape(8, 24, D)
    g1[:, :, 3840:] = as_columns(
        [columns(dbranch.astype(F32)), columns(dhidden * normed_one), columns(dhidden),
         down_bias_grad, gain_two_grad, shift_two_grad]
    ).reshape(32, 24, 128)
    for c, got, ss, rr in copies:
        remote(got, got, ss, rr, sibling).wait_recv()
        c.wait_send()


def middle(o, tokens, cotangent, w1, w2):
    return pl.pallas_call(
        middle_kernel,
        out_shape=(
            struct((T, D), BF), struct((T, D), F32), struct((4, T, 256), BF),
            struct((32,) + WIDE[1], BF), struct((32,) + WIDE[2], BF),
        ),
        in_specs=[VM, VM, VM, ANY, ANY],
        out_specs=(VM,) * 5,
        scratch_shapes=[
            pltpu.VMEM((4, T, 256), BF), pltpu.VMEM((4, T, 256), BF),
            pltpu.VMEM((32,) + WIDE[1], BF), pltpu.VMEM((32,) + WIDE[2], BF),
            pltpu.VMEM((4, 256, D), BF), pltpu.VMEM((4, T, D), BF), pltpu.VMEM((4, T, D), F32),
            DMA((2,)), DMA((3,)), DMA((3,)), DMA((3,)), DMA((3,)),
        ],
        compiler_params=pltpu.CompilerParams(collective_id=1, has_side_effects=True, vmem_limit_bytes=60 << 20),
        name="middle",
    )(o, tokens, cotangent, w1, w2)


def scatter_kernel(
    dq_ref, dkv_ref, tokens, dz1, w0, g1, g2, dx_ref, o0, o1, o2,
    wa, g0, a0, a1, a2, c0, c1, c2, b0, b1, b2, xs0, xs1, xs2, xr0, xr1, xr2, q_land, kv_land,
    load_sem, core_send, core_recv, send, recv, x_send, x_recv, q_send, q_recv, kv_send, kv_recv, w_sem,
):
    x, y, z, core = coords()
    grads, outs, acc, fro, buf = (g0, g1, g2), (o0, o1, o2), (a0, a1, a2), (c0, c1, c2), (b0, b1, b2)
    out_slabs, in_slabs = (xs0, xs1, xs2), (xr0, xr1, xr2)
    peers, rings, sibling = neighbours(x, y, z, core)
    others = across(x, y, z, core)
    fetch = pltpu.make_async_copy(w0, wa, w_sem.at[0])
    fetch.start()
    greet(peers + rings["y"] + rings["z"] + [sibling] + others)

    mine = (z % 2) * 4 + x
    copies = []
    for d in range(4):
        to = (1 - z % 2) * 4 + (x + d) % 4
        c = remote(dkv_ref.at[to], kv_land.at[mine], kv_send.at[4 + d], kv_recv.at[4 + d], others[d])
        c.start()
        copies.append((c, kv_land.at[(1 - z % 2) * 4 + (x + 4 - d) % 4], kv_send.at[4 + d], kv_recv.at[4 + d]))
    for d in (2, 1, 3):
        to, came = (x + d) % 4, (x + 4 - d) % 4
        c = remote(dkv_ref.at[(z % 2) * 4 + to], kv_land.at[mine], kv_send.at[d], kv_recv.at[d], peers[d - 1])
        c.start()
        copies.append((c, kv_land.at[(z % 2) * 4 + came], kv_send.at[d], kv_recv.at[d]))
        c = remote(dq_ref.at[to], q_land.at[x], q_send.at[d], q_recv.at[d], peers[d - 1])
        c.start()
        copies.append((c, q_land.at[came], q_send.at[d], q_recv.at[d]))
    kv_land[mine] = dkv_ref[mine]
    q_land[x] = dq_ref[x]

    def spot(route, a, b):
        dy, dz = (a, b) if ROUTES[route][0] == "yz" else (b, a)
        return dy, dz, dy * 4 + dz

    swaps, loads = {}, {}

    def begin_swaps(arrays):
        for b in (2, 1, 3, 0):
            for a in (2, 1, 3, 0):
                for r in BOTH:
                    dy, dz, at = spot(r, a, b)
                    here = block_of((y + dy) % 4, (z + dz) % 4, core)
                    there = block_of((y + dy) % 4, (z + dz) % 4, 1 - core)
                    for j, (k, first, cols) in enumerate(CHUNKS[r]):
                        if k not in arrays:
                            continue
                        n, view = (r * 16 + a * 4 + b) * 2 + j, pl.ds(first, cols)
                        swaps[n] = remote(
                            grads[k].at[there, :, view], fro[k].at[at, :, view], core_send.at[n], core_recv.at[n], sibling
                        )
                        loads[n] = pltpu.make_async_copy(grads[k].at[here, :, view], acc[k].at[at, :, view], load_sem.at[n])
                        swaps[n].start()
                        loads[n].start()

    begin_swaps((1, 2))
    fetch.wait()
    for c, got, ss, rr in copies:
        remote(got, got, ss, rr, sibling).wait_recv()
    dq = jnp.concatenate([q_land[g][:, 0:192].astype(F32) for g in range(4)], axis=1)
    both = [(kv_land[g].astype(F32) + kv_land[4 + g].astype(F32)) for g in range(4)]
    dk = jnp.concatenate([p for b in both for p in (b[:, 0:128], b[:, 256:320])], axis=1)
    dv = jnp.concatenate([p for b in both for p in (b[:, 128:256], b[:, 320:384])], axis=1)
    dqkv = jnp.concatenate([dq, dk, dv], axis=1).astype(BF)
    g0[:, :, : 3 * D] = dot_rows(tokens[...], dqkv).astype(BF).reshape(32, 24, 3 * D)
    bias = jnp.sum(dqkv.astype(F32), axis=0, keepdims=True)
    bias = jnp.concatenate([bias[:, :D], bias[:, 2 * D :], jnp.zeros((126, D), F32)], axis=0)
    g0[:, :, 3 * D :] = bias.T.astype(BF).reshape(32, 24, 128)
    begin_swaps((0,))
    dx_ref[...] = dz1[...] + dot_t(dqkv, wa[...].reshape(D, NA)[:, : 3 * D])

    def fold(r, a, b):
        _, _, at = spot(r, a, b)
        for j, (k, first, cols) in enumerate(CHUNKS[r]):
            n = (r * 16 + a * 4 + b) * 2 + j
            loads[n].wait()
            swaps[n].wait_recv()
            view = (at, slice(None), pl.ds(first, cols))
            acc[k][view] = acc[k][view] + fro[k][view]

    started = []

    def slot(r, group, kind, i):
        return (r * 5 + group) * 9 + kind * 3 + (len(ROUTES[r][1][0]) if i else 0)

    def axis(r, group):
        return rings[ROUTES[r][0][0 if group == 0 else 1]]

    def at_of(r, group, step):
        return spot(r, *((step, 0) if group == 0 else (group - 1, step)))[2]

    def push(r, group, kind, i, step, who):
        for j, (k, first, cols) in enumerate(ROUTES[r][1][i]):
            n, view = slot(r, group, kind, i) + j, pl.ds(first, cols)
            c = remote(
                acc[k].at[at_of(r, group, step), :, view], buf[k].at[group * 3 + kind, :, view], send.at[n], recv.at[n], who
            )
            c.start()
            started.append(c)

    def add(r, group, kind, i, step):
        for j, (k, first, cols) in enumerate(ROUTES[r][1][i]):
            n, view = slot(r, group, kind, i) + j, pl.ds(first, cols)
            got = buf[k].at[group * 3 + kind, :, view]
            remote(got, got, send.at[n], recv.at[n], sibling).wait_recv()
            at = (at_of(r, group, step), slice(None), view)
            acc[k][at] = acc[k][at] + buf[k][group * 3 + kind, :, view]

    def first_step(r, group):
        right, left = axis(r, group)
        push(r, group, 0, 0, 2, right)
        push(r, group, 0, 1, 2, left)

    def second_step(r, group):
        right, left = axis(r, group)
        add(r, group, 0, 0, 1)
        push(r, group, 1, 0, 1, right)
        push(r, group, 1, 1, 1, right)
        add(r, group, 0, 1, 3)
        push(r, group, 2, 0, 3, left)
        push(r, group, 2, 1, 3, left)

    def third_step(r, group):
        for kind in (1, 2):
            for i in BOTH:
                add(r, group, kind, i, 0)

    turns = (2, 1, 3, 0)
    for a in turns:
        for r in BOTH:
            fold(r, a, 2)
            first_step(r, 1 + a)
    for a in turns:
        for r in BOTH:
            fold(r, a, 1)
            fold(r, a, 3)
            second_step(r, 1 + a)
    for a in turns:
        for r in BOTH:
            fold(r, a, 0)
            third_step(r, 1 + a)
            if a == 2:
                first_step(r, 0)
            if a == 3:
                second_step(r, 0)
    for r in BOTH:
        third_step(r, 0)

    x_copies = []
    for d in (2, 1, 3):
        for k, rows in enumerate(ROWS):
            pick = picker((TALL[k][0], 4 * rows), rows, (x + d) % 4, True)
            out_slabs[k][d - 1] = dot(pick, acc[k][0]).astype(BF)
            c = remote(out_slabs[k].at[d - 1], in_slabs[k].at[d - 1], x_send.at[d - 1, k], x_recv.at[d - 1, k], peers[d - 1])
            c.start()
            x_copies.append(c)
    for k, rows in enumerate(ROWS):
        outs[k][...] = dot(picker((TALL[k][0], 4 * rows), rows, x, True), acc[k][0])
    for c in x_copies:
        c.wait_recv()
    for k in range(3):
        outs[k][...] += in_slabs[k][0].astype(F32) + in_slabs[k][1].astype(F32) + in_slabs[k][2].astype(F32)
    for c in x_copies + started + list(swaps.values()) + [c for c, _, _, _ in copies]:
        c.wait_send()


def scatter_grads(dq, dkv, tokens, dz1, w0, g1, g2):
    return pl.pallas_call(
        scatter_kernel,
        out_shape=(struct((T, D), F32),) + tuple(struct(t, F32) for t in TALL),
        in_specs=[VM, VM, VM, VM, ANY, ANY, ANY],
        out_specs=(VM,) * 4,
        scratch_shapes=[pltpu.VMEM((32,) + WIDE[0], BF)] * 2
        + [pltpu.VMEM((16,) + w, BF) for w in WIDE] * 2
        + [pltpu.VMEM((15,) + w, BF) for w in WIDE]
        + [pltpu.VMEM((3,) + t, BF) for t in TALL] * 2
        + [pltpu.VMEM((4, T, 256), BF), pltpu.VMEM((8, T, 384), BF)]
        + [DMA((64,)), DMA((64,)), DMA((64,)), DMA((90,)), DMA((90,)), DMA((3, 3)), DMA((3, 3))]
        + [DMA((4,)), DMA((4,)), DMA((8,)), DMA((8,)), DMA((1,))],
        compiler_params=pltpu.CompilerParams(collective_id=2, has_side_effects=True, vmem_limit_bytes=62 << 20),
        name="scatter_grads",
    )(dq, dkv, tokens, dz1, w0, g1, g2)


def shards(
    tokens, lengths, block_table, qkv_weight, query_bias, value_bias, out_weight, out_bias, first_gain, first_shift,
    up_weight, up_bias, down_weight, down_bias, second_gain, second_shift, cotangent,
):
    def pack(arrays, shape):
        wide = jnp.concatenate([a if a.ndim == 2 else a[:, None] for a in arrays], axis=1)
        return jnp.pad(wide, ((0, shape[0] - wide.shape[0]), (0, shape[1] - wide.shape[1])))

    slabs = (
        pack((qkv_weight, query_bias, value_bias), TALL[0]),
        pack((out_weight, up_weight, out_bias, first_gain, first_shift, down_bias, second_gain, second_shift), TALL[1]),
        pack((down_weight, up_bias), TALL[2]),
    )
    ends = jnp.cumsum(lengths[0])
    block_seg = jnp.sum((block_table[0][:, None] >= ends[None, :]).astype(jnp.int32), axis=1)
    seg = jnp.repeat(block_seg, 128)
    half = lax.dynamic_slice_in_dim(seg, (lax.axis_index("seq") // 4) * 1024, 1024)
    w0, w1, w2, q, kv = gather_weights(*slabs, tokens)
    q, kv = q.reshape(1024, 256), kv.reshape(2048, 384)
    o, lse = attend(q, kv, jnp.broadcast_to(half[:, None], (1024, 128)), jnp.broadcast_to(seg[None, :], (8, 2048)))
    result, dz1, do, g1, g2 = middle(o.reshape(4, T, 256), tokens, cotangent, w1, w2)
    dq, dkv = attend_back(
        q, kv, do.reshape(1024, 256), o, lse,
        jnp.broadcast_to(half[None, :], (8, 1024)), jnp.broadcast_to(seg[:, None], (2048, 128)),
    )
    dx, ga, gb, gc = scatter_grads(dq.reshape(4, T, 256), dkv.reshape(8, T, 384), tokens, dz1, w0, g1, g2)
    vectors = gb[:6, 3840:3846]
    return (
        result, dx, ga[:6, : 3 * D], ga[:6, 3 * D], ga[:6, 3 * D + 1],
        gb[:6, :D], vectors[:, 0], vectors[:, 1], vectors[:, 2],
        gb[:6, D:3840], gc[:24, D], gc[:24, :D], vectors[:, 3], vectors[:, 4], vectors[:, 5],
    )


def solution(mesh):
    both = ("fsdp", "seq")
    whole, flat, group = P(both, None), P(both), P("fsdp", None)
    return jax.shard_map(
        shards,
        mesh=mesh,
        in_specs=(whole, group, group, whole, flat, flat, whole, flat, flat, flat, whole, flat, whole, flat, flat, flat, whole),
        out_specs=(whole, whole, whole, flat, flat, whole, flat, flat, flat, whole, flat, whole, flat, flat, flat),
        check_vma=False,
    )
```

time: 2430 us -> 291 us (0.12)
  waiting for transfers between devices: 1250 us -> 0 us
  blocking collectives: 520 us -> 0 us
  Pallas kernels: 0 us -> 262 us
  matrix products: 205 us -> 0 us
  local copies, waits for them, and re-layouts: 209 us -> 25.2 us
  starting transfers between devices: 183 us -> 0 us
  other arithmetic: 35 us -> 2.34 us
    all_gather x6 -> x0, waiting for transfers between devices: 1110 us -> none  [the longest x1 310 us: shards(): lax.all_gather(qkv_weight, ('fsdp', 'seq'), axis=0, tiled=True)]
    unnamed x3 -> x0, blocking collectives: 520 us -> none
    pallas_call x0 -> x5, Pallas kernels: none -> 262 us  [the longest x1 96.7 us: gather_weights(): pl.pallas_call(gather_kernel, out_shape=tuple((struct((32,) + w, BF) for...]
    dot_general x96 -> x0, matrix products: 205 us -> none  [the longest x12 27.3 us: attend(): out = jnp.dot(probs, v_head, preferred_element_type=jnp.float32)]
    unnamed x65 -> x0, starting transfers between devices: 182 us -> none
    unnamed x173 -> x14, local copies, waits for them, and re-layouts: 167 us -> 5.4 us
    reduce_scatter x3 -> x0, waiting for transfers between devices: 141 us -> none  [the longest x1 48.3 us: shards(): lax.psum_scatter(join_heads(grad_kh).astype(jnp.bfloat16), 'seq', scatter...]
  transfers between devices with their start and end apart: 74 -> 0, of which waited for: 11 -> 0; matrix products, arithmetic and copies ran while one was open for 28% -> 0% of each run, Pallas kernels for 0% -> 0%
where the time goes in v1:
time: 291 us; the launch traced here: 290 us
  Pallas kernels  262 us (90%)
  local copies, waits for them, and re-layouts  25.2 us (9%)
    pallas_call x1, Pallas kernels, gather_weights(): pl.pallas_call(gather_kernel, out_shape=tuple((struct((32,) + w, BF) for...  96.7 us
    pallas_call x1, Pallas kernels, scatter_grads(): pl.pallas_call(scatter_kernel, out_shape=(struct((T, D), F32),) + tuple((...  96.5 us
    pallas_call x1, Pallas kernels, middle(): pl.pallas_call(middle_kernel, out_shape=(struct((T, D), BF), struct((T, D...  34.4 us
    pallas_call x1, Pallas kernels, attend_back(): pl.pallas_call(attend_back_kernel, grid=(1024 // step,), out_shape=(struc...  21.9 us
    pallas_call x1, Pallas kernels, attend(): pl.pallas_call(attend_kernel, grid=(1024 // step,), out_shape=(struct((10...  12.1 us
    broadcast_in_dim x9, local copies, waits for them, and re-layouts, pack(): a[:, None]  6.79 us

profile of v1, /device:TPU:0, one launch (start us, length us, event | category | flops | bytes accessed | tf_op | source)
XLA Modules:
  0.0 290.1 jit_solution(13558072870742510714)
XLA Ops:
  0.7 0.8 reduce-window.8
  1.5 0.7 convert_reduce_fusion
  2.2 0.1 broadcast_bitcast_fusion
  2.3 0.2 broadcast_in_dim.63.qseg
  2.5 0.8 copy.52
  3.3 0.8 copy.53
  4.0 0.8 copy.54
  4.8 0.8 copy.55
  5.5 0.8 copy.56
  6.3 0.8 copy.57
  7.0 0.9 concatenate.10
  8.0 0.8 copy.50
  8.7 0.8 copy.51
  9.5 0.9 concatenate.9
  10.3 0.7 copy.58
  11.1 0.8 fusion.5.s2
  11.9 0.0 copy-start.1
  11.9 1.0 copy-done.1
  12.9 96.7 %gather_weights.1 = (bf16[32,24,2432]{2,1,0:T(8,128)(2,1)}, bf16[32,24,3968]{2,1,0:T(8,128)(2,1)}, bf16[32,96,896]{2,1,0:T(8,128)(2,1)}, bf16[4,256,256]{2,1,0:T(8,128)(2,1)S(1)}, bf16[8,256,384]{2,1,0:T(8,128)(2,1)S(1)}) custom-call(bf16[16,2432]{1,0:T(8,128)(2,1)S(1)} %pad.12.s0, bf16[16,3968]{1,0:T(8,128)(2,1)S(1)} %pad.13.s1, ...), custom_call_target="tpu_custom_call" | custom-call | tf_op jit(solution)/shard_map/gather_weights/pallas_call | solution.py:266
  109.6 0.0 copy-start
  109.6 0.0 copy-start.3
  109.6 12.1 %attend.1 = (bf16[1024,256]{1,0:T(8,128)(2,1)S(1)}, f32[1024,128]{1,0:T(8,128)S(1)}) custom-call(bf16[1024,256]{1,0:T(8,128)(2,1)S(1)} %bitcast.23, bf16[2048,384]{1,0:T(8,128)(2,1)S(1)} %bitcast.20, s32[1024,128]{1,0:T(8,128)S(1)} %broadcast_in_dim.63.qseg, s32[8,2048]{1,0:T(8,128)S(1)} %broadcast_in_dim.64.kseg), custom_call_target="tpu_custom_call" | custom-call | tf_op jit(solution)/shard_map/attend/pallas_call | solution.py:312
  121.8 0.0 copy-start.2
  121.8 0.8 copy-done.2
  122.6 0.0 copy-start.4
  122.6 0.8 copy-done.4
  123.4 34.4 %middle.1 = (bf16[256,768]{1,0:T(8,128)(2,1)}, f32[256,768]{1,0:T(8,128)}, bf16[4,256,256]{2,1,0:T(8,128)(2,1)}, bf16[32,24,3968]{2,1,0:T(8,128)(2,1)}, bf16[32,96,896]{2,1,0:T(8,128)(2,1)}) custom-call(bf16[4,256,256]{2,1,0:T(8,128)(2,1)} %bitcast.22, bf16[256,768]{1,0:T(8,128)(2,1)} %tokens.5, bf16[256,768]{1,0:T(8,128)(2,1)} %cotangent.1, ...), custom_call_target="tpu_custom_call" | custom-call | tf_op jit(solution)/shard_map/middle/pallas_call | solution.py:499
  157.8 0.0 copy-done
  157.8 0.0 copy-done.3
  157.8 0.6 broadcast_in_dim.65.qseg
  158.5 1.3 broadcast_in_dim.66.kseg
  159.8 21.9 %attend_back.1 = (bf16[1024,256]{1,0:T(8,128)(2,1)}, bf16[2048,384]{1,0:T(8,128)(2,1)}) custom-call(bf16[1024,256]{1,0:T(8,128)(2,1)} %bitcast.24, bf16[2048,384]{1,0:T(8,128)(2,1)} %bitcast.21, bf16[1024,256]{1,0:T(8,128)(2,1)} %bitcast.26, bf16[1024,256]{1,0:T(8,128)(2,1)} %copy-done.2, f32[1024,128]{1,0:T(8,128)} %copy-done.4, ...), custom_call_target="tpu_custom_call" | custom-call | tf_op jit(solution)/shard_map/attend_back/pallas_call | solution.py:372
  181.7 0.0 copy-start.5
  181.7 96.5 %scatter_grads.1 = (f32[256,768]{1,0:T(8,128)}, f32[16,2432]{1,0:T(8,128)}, f32[16,3968]{1,0:T(8,128)}, f32[32,896]{1,0:T(8,128)}) custom-call(bf16[4,256,256]{2,1,0:T(8,128)(2,1)} %bitcast.27, bf16[8,256,384]{2,1,0:T(8,128)(2,1)} %bitcast.25, bf16[256,768]{1,0:T(8,128)(2,1)} %tokens.5, f32[256,768]{1,0:T(8,128)} %get-tuple-element.43.dz1, ...), custom_call_target="tpu_custom_call" | custom-call | tf_op jit(solution)/shard_map/scatter_grads/pallas_call | solution.py:686
  278.3 1.7 slice_reduce_fusion.1
  280.0 1.5 slice.53
  281.5 1.5 slice.46
  283.1 1.5 slice.55
  284.6 1.3 slice.49
  285.9 1.3 slice_reduce_fusion
  287.3 0.0 copy-done.5
  287.3 0.7 copy.61
  288.0 2.1 copy.62
  (4 shorter events, 0.0 us)
Async XLA Ops:
  11.9 1.0 copy-start.1
  109.6 48.2 %copy-start = (bf16[8,256,384]{2,1,0:T(8,128)(2,1)}, bf16[8,256,384]{2,1,0:T(8,128)(2,1)S(1)}, u32[]{:S(2)}) copy-start(bf16[8,256,384]{2,1,0:T(8,128)(2,1)S(1)} %get-tuple-element.34) | copy-start | bytes 4718596
  109.6 48.2 %copy-start.3 = (bf16[4,256,256]{2,1,0:T(8,128)(2,1)}, bf16[4,256,256]{2,1,0:T(8,128)(2,1)S(1)}, u32[]{:S(2)}) copy-start(bf16[4,256,256]{2,1,0:T(8,128)(2,1)S(1)} %get-tuple-element.33) | copy-start | bytes 1572868
  121.8 0.8 copy-start.2
  122.6 0.8 copy-start.4
  181.7 105.5 %copy-start.5 = (bf16[256,768]{1,0:T(8,128)(2,1)S(1)}, bf16[256,768]{1,0:T(8,128)(2,1)}, u32[]{:S(2)}) copy-start(bf16[256,768]{1,0:T(8,128)(2,1)} %get-tuple-element.76) | copy-start | bytes 1179652
